TPU v7x, 32 devices: a whole 2x2x4 slice. The times are simulated.
32 devices in a mesh: src: 4 (over z), tgt: 8 (over y, x, core).
Axes of the slice: x: 2, y: 2, z: 4, core: 2. Of those that a mesh axis runs over, the one named last changes fastest.
Arguments:
- coupling: bfloat16 [2048, 4096], P('src', 'tgt'), may hold values from 0.25 to 4
- src_pcs: bfloat16 [50, 2048], P(None, 'src'), may hold values from -24 to 24
- tgt_pcs: bfloat16 [50, 4096], P(None, 'tgt'), may hold values from -24 to 24
- src_mass: float32 [2048], P('src'), may hold values from 0.25 to 4
- tgt_mass: float32 [4096], P('tgt'), may hold values from 0.25 to 4
Outputs:
- log_coupling: float32 [2048, 4096], P('src', 'tgt')
- row_potential: float32 [2048], P('src')
- col_potential: float32 [4096], P('tgt')
All inputs are finite; a program needn't handle non-finite values.
Results may differ from a plain program's by a relative error of at most 0.0019.
Values sent between devices are 32-bit elements; how exact they have to be, the bound alone decides.
No kernel may reach another device: no remote copies, remote signals or barrier semaphores. Data moves between devices by JAX's collectives and lax.ppermute only.
A program may use at most 64 MiB of HBM per device.

v0:
```python
import jax
import jax.numpy as jnp
from jax import lax
from jax.sharding import PartitionSpec as P

PCS = 50
ITERS = 4


eps_reg = 0.5
marg_power = 1.0 / (1.0 + eps_reg)
tiny_eps = 1e-06


def row_logmean(shifted, count):
    local_max = jnp.max(shifted, axis=1)
    highest = lax.pmax(local_max, "tgt")
    summed_exp = lax.psum(jnp.sum(jnp.exp(shifted - highest[:, None]), axis=1), "tgt")
    return highest + jnp.log(summed_exp) - jnp.log(jnp.float32(count))


def col_logmean(shifted, count):
    local_max = jnp.max(shifted, axis=0)
    highest = lax.pmax(local_max, "src")
    summed_exp = lax.psum(jnp.sum(jnp.exp(shifted - highest[None, :]), axis=0), "src")
    return highest + jnp.log(summed_exp) - jnp.log(jnp.float32(count))


def shards(coupling, src_pcs, tgt_pcs, src_mass, tgt_mass):
    exact = lax.Precision.HIGHEST
    total_rows = coupling.shape[0] * lax.axis_size("src")
    total_cols = coupling.shape[1] * lax.axis_size("tgt")
    src_float = src_pcs.astype(jnp.float32)
    tgt_float = tgt_pcs.astype(jnp.float32)
    block_panel = jnp.dot(src_pcs, coupling, preferred_element_type=jnp.float32)
    block_moment = jnp.dot(block_panel, tgt_float.T, precision=exact)
    moment = lax.psum(block_moment, ("src", "tgt"))
    moment = moment * (total_rows * total_cols) ** (-0.5)
    normed = moment / jnp.sqrt(jnp.mean(moment * moment) + tiny_eps)
    weighted = jnp.dot(normed, tgt_float, precision=exact)
    scores = jnp.dot(src_float.T, weighted, precision=exact) * (2.0 / (eps_reg * PCS))
    log_src = jnp.log(src_mass)
    log_tgt = jnp.log(tgt_mass)
    col_potential = jnp.zeros((coupling.shape[1],), jnp.float32)
    row_potential = jnp.zeros((coupling.shape[0],), jnp.float32)
    for iteration in range(ITERS):
        row_potential = marg_power * (
            log_src - row_logmean(scores + col_potential[None, :], total_cols)
        )
        col_potential = marg_power * (
            log_tgt - col_logmean(scores + row_potential[:, None], total_rows)
        )
    log_coupling = scores + row_potential[:, None] + col_potential[None, :]
    return (log_coupling, row_potential, col_potential)


def solution(mesh):
    in_specs = (P("src", "tgt"), P(None, "src"), P(None, "tgt"), P("src"), P("tgt"))
    out_specs = (P("src", "tgt"), P("src"), P("tgt"))
    return jax.shard_map(shards, mesh=mesh, in_specs=in_specs, out_specs=out_specs, check_vma=False)
```

profile of v0, /device:TPU:0, one launch (start us, length us, event | category | flops | bytes accessed | tf_op | source)
XLA Modules:
  0.0 223.9 jit_solution(8890116766683213945)
XLA Ops:
  0.7 1.0 copy-done
  1.7 1.0 fusion.7
  2.9 42.3 %psum.63 = f32[50,50]{1,0:T(8,128)S(1)} all-reduce(f32[50,50]{1,0:T(8,128)S(1)} %fusion.8), channel_id=1, replica_groups=mesh['src'=4,'tgt'=8] {'src','tgt'}, use_global_device_ids=true, to_apply=%region_0.0 | all-reduce | flops 2500 | bytes 20000 | tf_op jit(solution)/shard_map/psum | solution.py:37
  45.2 0.6 multiply_reduce_fusion
  46.7 0.6 copy-done.2
  47.3 0.7 fusion.6
  48.0 12.8 %pmax.56 = f32[512]{0:T(512)S(1)} all-reduce(f32[512]{0:T(512)S(1)} %get-tuple-element.6), channel_id=1, replica_groups=mesh['src'=4,'tgt'=8] {'tgt'}, use_global_device_ids=true, to_apply=%region_3.0 | all-reduce | flops 512 | bytes 4096 | tf_op jit(solution)/shard_map/pmax | solution.py:17
  60.8 0.2 exponential_reduce_fusion.7
  61.0 11.8 %psum.64 = f32[512]{0:T(512)S(1)} all-reduce(f32[512]{0:T(512)S(1)} %exponential_reduce_fusion.7), channel_id=1, replica_groups=mesh['src'=4,'tgt'=8] {'tgt'}, use_global_device_ids=true, to_apply=%region_5.0 | all-reduce | flops 512 | bytes 4096 | tf_op jit(solution)/shard_map/psum | solution.py:18
  72.9 10.6 %pmax.57 = f32[512]{0:T(512)S(1)} all-reduce(f32[512]{0:T(512)S(1)} %add_reduce_fusion.5), channel_id=1, replica_groups=mesh['src'=4,'tgt'=8] {'src'}, use_global_device_ids=true, to_apply=%region_7.0 | all-reduce | flops 512 | bytes 4096 | tf_op jit(solution)/shard_map/pmax | solution.py:24
  83.5 0.3 exponential_reduce_fusion.6
  83.8 8.4 %psum.65 = f32[512]{0:T(512)S(1)} all-reduce(f32[512]{0:T(512)S(1)} %exponential_reduce_fusion.6), channel_id=1, replica_groups=mesh['src'=4,'tgt'=8] {'src'}, use_global_device_ids=true, to_apply=%region_9.0 | all-reduce | flops 512 | bytes 4096 | tf_op jit(solution)/shard_map/psum | solution.py:25
  92.3 11.8 %pmax.58 = f32[512]{0:T(512)S(1)} all-reduce(f32[512]{0:T(512)S(1)} %add_reduce_fusion.4), channel_id=1, replica_groups=mesh['src'=4,'tgt'=8] {'tgt'}, use_global_device_ids=true, to_apply=%region_11.0 | all-reduce | flops 512 | bytes 4096 | tf_op jit(solution)/shard_map/pmax | solution.py:17
  104.1 0.3 exponential_reduce_fusion.5
  104.4 11.8 %psum.66 = f32[512]{0:T(512)S(1)} all-reduce(f32[512]{0:T(512)S(1)} %exponential_reduce_fusion.5), channel_id=1, replica_groups=mesh['src'=4,'tgt'=8] {'tgt'}, use_global_device_ids=true, to_apply=%region_13.0 | all-reduce | flops 512 | bytes 4096 | tf_op jit(solution)/shard_map/psum | solution.py:18
  116.4 10.4 %pmax.59 = f32[512]{0:T(512)S(1)} all-reduce(f32[512]{0:T(512)S(1)} %add_reduce_fusion.3), channel_id=1, replica_groups=mesh['src'=4,'tgt'=8] {'src'}, use_global_device_ids=true, to_apply=%region_15.0 | all-reduce | flops 512 | bytes 4096 | tf_op jit(solution)/shard_map/pmax | solution.py:24
  126.7 0.3 exponential_reduce_fusion.4
  127.1 8.4 %psum.67 = f32[512]{0:T(512)S(1)} all-reduce(f32[512]{0:T(512)S(1)} %exponential_reduce_fusion.4), channel_id=1, replica_groups=mesh['src'=4,'tgt'=8] {'src'}, use_global_device_ids=true, to_apply=%region_17.0 | all-reduce | flops 512 | bytes 4096 | tf_op jit(solution)/shard_map/psum | solution.py:25
  135.6 11.8 %pmax.60 = f32[512]{0:T(512)S(1)} all-reduce(f32[512]{0:T(512)S(1)} %add_reduce_fusion.2), channel_id=1, replica_groups=mesh['src'=4,'tgt'=8] {'tgt'}, use_global_device_ids=true, to_apply=%region_19.0 | all-reduce | flops 512 | bytes 4096 | tf_op jit(solution)/shard_map/pmax | solution.py:17
  147.4 0.3 exponential_reduce_fusion.3
  147.7 11.8 %psum.68 = f32[512]{0:T(512)S(1)} all-reduce(f32[512]{0:T(512)S(1)} %exponential_reduce_fusion.3), channel_id=1, replica_groups=mesh['src'=4,'tgt'=8] {'tgt'}, use_global_device_ids=true, to_apply=%region_21.0 | all-reduce | flops 512 | bytes 4096 | tf_op jit(solution)/shard_map/psum | solution.py:18
  159.6 10.4 %pmax.61 = f32[512]{0:T(512)S(1)} all-reduce(f32[512]{0:T(512)S(1)} %add_reduce_fusion.1), channel_id=1, replica_groups=mesh['src'=4,'tgt'=8] {'src'}, use_global_device_ids=true, to_apply=%region_23.0 | all-reduce | flops 512 | bytes 4096 | tf_op jit(solution)/shard_map/pmax | solution.py:24
  170.0 0.3 exponential_reduce_fusion.2
  170.3 8.4 %psum.69 = f32[512]{0:T(512)S(1)} all-reduce(f32[512]{0:T(512)S(1)} %exponential_reduce_fusion.2), channel_id=1, replica_groups=mesh['src'=4,'tgt'=8] {'src'}, use_global_device_ids=true, to_apply=%region_25.0 | all-reduce | flops 512 | bytes 4096 | tf_op jit(solution)/shard_map/psum | solution.py:25
  178.9 11.8 %pmax.62 = f32[512]{0:T(512)S(1)} all-reduce(f32[512]{0:T(512)S(1)} %add_reduce_fusion), channel_id=1, replica_groups=mesh['src'=4,'tgt'=8] {'tgt'}, use_global_device_ids=true, to_apply=%region_27.0 | all-reduce | flops 512 | bytes 4096 | tf_op jit(solution)/shard_map/pmax | solution.py:17
  190.7 0.3 exponential_reduce_fusion.1
  190.9 11.8 %psum.70 = f32[512]{0:T(512)S(1)} all-reduce(f32[512]{0:T(512)S(1)} %exponential_reduce_fusion.1), channel_id=1, replica_groups=mesh['src'=4,'tgt'=8] {'tgt'}, use_global_device_ids=true, to_apply=%region_29.0 | all-reduce | flops 512 | bytes 4096 | tf_op jit(solution)/shard_map/psum | solution.py:18
  202.9 10.4 %pmax.63 = f32[512]{0:T(512)S(1)} all-reduce(f32[512]{0:T(512)S(1)} %add_reduce_fusion.6), channel_id=1, replica_groups=mesh['src'=4,'tgt'=8] {'src'}, use_global_device_ids=true, to_apply=%region_31.0 | all-reduce | flops 512 | bytes 4096 | tf_op jit(solution)/shard_map/pmax | solution.py:24
  213.3 0.3 exponential_reduce_fusion
  213.6 8.4 %psum.71 = f32[512]{0:T(512)S(1)} all-reduce(f32[512]{0:T(512)S(1)} %exponential_reduce_fusion), channel_id=1, replica_groups=mesh['src'=4,'tgt'=8] {'src'}, use_global_device_ids=true, to_apply=%region_33.0 | all-reduce | flops 512 | bytes 4096 | tf_op jit(solution)/shard_map/psum | solution.py:25
  222.1 0.4 copy-done.6
  222.6 1.3 copy.8
  (29 shorter events, 1.7 us)
Async XLA Ops:
  0.6 1.0 copy-start
  0.6 2.1 copy-start.1
  46.5 0.8 copy-start.2
  60.8 12.0 %copy-start.3 = (f32[512]{0:T(512)S(1)}, f32[512]{0:T(512)}, u32[]{:S(2)}) copy-start(f32[512]{0:T(512)} %param.8) | copy-start | bytes 6148
  83.5 8.7 %copy-start.4 = (f32[512]{0:T(512)S(1)}, f32[512]{0:T(512)}, u32[]{:S(2)}) copy-start(f32[512]{0:T(512)} %param.9) | copy-start | bytes 6148
  202.7 19.2 %copy-start.5 = (f32[512]{0:T(512)}, f32[512]{0:T(512)S(1)}, u32[]{:S(2)}) copy-start(f32[512]{0:T(512)S(1)} %subtract_multiply_fusion.1) | copy-start | bytes 6148
  222.0 0.6 copy-start.6
where the time goes:
time: 225 us; the launch traced here: 224 us
  blocking collectives  213 us (95%)
  other arithmetic  4.18 us (2%)
  local copies, waits for them, and re-layouts  3.4 us (2%)
    pmax x4, blocking collectives, row_logmean(): highest = lax.pmax(local_max, 'tgt')  48.2 us
    psum x4, blocking collectives, row_logmean(): lax.psum(jnp.sum(jnp.exp(shifted - highest[:, None]), axis=1), 'tgt')  47.2 us
    psum x1, blocking collectives, shards(): moment = lax.psum(block_moment, ('src', 'tgt'))  42.3 us
    pmax x4, blocking collectives, col_logmean(): highest = lax.pmax(local_max, 'src')  41.7 us
    psum x4, blocking collectives, col_logmean(): lax.psum(jnp.sum(jnp.exp(shifted - highest[None, :]), axis=0), 'src')  33.5 us

commit v1 on v0

v1 whole, which is shorter than its diff:
```python
import functools

import jax
import jax.numpy as jnp
from jax import lax
from jax.sharding import PartitionSpec as P

PCS = 50
ITERS = 4


eps_reg = 0.5
marg_power = 1.0 / (1.0 + eps_reg)
tiny_eps = 1e-06

RADIX = 8


def exchange(value, axis, low, span):
    size = lax.axis_size(axis)
    out = [value]
    for j in range(1, span):
        perm = [(i, i ^ (low * j)) for i in range(size)]
        out.append(lax.ppermute(value, axis, perm))
    return out


def tree(values, combine):
    while len(values) > 1:
        values = [combine(values[i], values[i + 1]) for i in range(0, len(values), 2)]
    return values[0]


def stages(axis):
    size = lax.axis_size(axis)
    low = 1
    while low < size:
        span = min(RADIX, size // low)
        yield low, span
        low *= span


def all_sum(value, axis):
    for low, span in stages(axis):
        value = tree(exchange(value, axis, low, span), jnp.add)
    return value


def all_logsum(value, axis):
    for low, span in stages(axis):
        parts = exchange(value, axis, low, span)
        highest = tree(parts, jnp.maximum)
        total = tree([jnp.exp(part - highest) for part in parts], jnp.add)
        value = highest + jnp.log(total)
    return value


def all_blocks(value, axis):
    blocks = [value]
    for low, span in stages(axis):
        fresh = [exchange(block, axis, low, span) for block in blocks]
        blocks = [fresh[b][j] for j in range(span) for b in range(len(blocks))]
    return blocks


def shards(coupling, src_pcs, tgt_pcs, src_mass, tgt_mass):
    exact = lax.Precision.HIGHEST
    total_rows = coupling.shape[0] * lax.axis_size("src")
    total_cols = coupling.shape[1] * lax.axis_size("tgt")
    src_float = src_pcs.astype(jnp.float32)
    tgt_float = tgt_pcs.astype(jnp.float32)
    packed = jnp.concatenate([src_float, src_mass[None, :]], axis=0)
    src_blocks = all_blocks(packed, "src")
    block_panel = jnp.dot(src_pcs, coupling, preferred_element_type=jnp.float32)
    block_moment = jnp.dot(block_panel, tgt_float.T, precision=exact)
    moment = all_sum(all_sum(block_moment, "tgt"), "src")
    moment = moment * (total_rows * total_cols) ** (-0.5)
    normed = moment / jnp.sqrt(jnp.mean(moment * moment) + tiny_eps)
    weighted = jnp.dot(normed, tgt_float, precision=exact) * (2.0 / (eps_reg * PCS))
    everything = jnp.concatenate(src_blocks, axis=1)
    src_all = everything[:PCS]
    log_src = jnp.log(everything[PCS]) + jnp.log(jnp.float32(total_cols))
    log_tgt = jnp.log(tgt_mass) + jnp.log(jnp.float32(total_rows))
    scores = jnp.dot(src_all.T, weighted, precision=exact)
    col_potential = jnp.zeros((coupling.shape[1],), jnp.float32)
    blocks = len(src_blocks)
    rows = coupling.shape[0]
    for iteration in range(ITERS):
        shifted = scores + col_potential[None, :]
        highest = jnp.max(shifted, axis=1)
        summed = jnp.sum(jnp.exp(shifted - highest[:, None]), axis=1)
        row_potential = marg_power * (log_src - all_logsum(highest + jnp.log(summed), "tgt"))
        shifted = (scores + row_potential[:, None]).reshape(blocks, rows, -1)
        highest = jnp.max(shifted, axis=(0, 1))
        sums = jnp.sum(jnp.exp(shifted - highest[None, None, :]), axis=1)
        summed = tree([sums[b] for b in range(blocks)], jnp.add)
        col_potential = marg_power * (log_tgt - (highest + jnp.log(summed)))
    row_potential = row_potential[:rows]
    log_coupling = scores[:rows] + row_potential[:, None] + col_potential[None, :]
    return (log_coupling, row_potential, col_potential)


def solution(mesh):
    in_specs = (P("src", "tgt"), P(None, "src"), P(None, "tgt"), P("src"), P("tgt"))
    out_specs = (P("src", "tgt"), P("src"), P("tgt"))
    return jax.shard_map(shards, mesh=mesh, in_specs=in_specs, out_specs=out_specs, check_vma=False)
```

time: 225 us -> 83.2 us (0.37)
  blocking collectives: 213 us -> 0 us
  starting transfers between devices: 0 us -> 41.1 us
  waiting for transfers between devices: 0 us -> 17.5 us
  other arithmetic: 4.18 us -> 14.7 us
  matrix products: 2.04 us -> 6.62 us
  local copies, waits for them, and re-layouts: 3.4 us -> 1.14 us
    psum x9 -> x0, blocking collectives: 123 us -> none  [the longest x4 47.2 us: row_logmean(): lax.psum(jnp.sum(jnp.exp(shifted - highest[:, None]), axis=1), 'tgt')]
    pmax x8 -> x0, blocking collectives: 89.9 us -> none  [the longest x4 48.2 us: row_logmean(): highest = lax.pmax(local_max, 'tgt')]
    ppermute x0 -> x41, starting transfers between devices: none -> 41.1 us  [exchange(): out.append(lax.ppermute(value, axis, perm))]
    ppermute x0 -> x41, waiting for transfers between devices: none -> 17.5 us  [exchange(): out.append(lax.ppermute(value, axis, perm))]
    reduce_sum x8, other arithmetic: 2.23 us -> 7.7 us  [the longest x4 5.41 us: shards(): summed = jnp.sum(jnp.exp(shifted - highest[:, None]), axis=1)]
    dot_general x2, matrix products: 0.84 us -> 4.6 us  [the longest x1 3.6 us: shards(): scores = jnp.dot(src_all.T, weighted, precision=exact)]
    unnamed x15 -> x10, local copies, waits for them, and re-layouts: 3.4 us -> 1.14 us
  transfers between devices with their start and end apart: 0 -> 41, of which waited for: 0 -> 16; matrix products, arithmetic and copies ran while one was open for 0% -> 4% of each run, Pallas kernels for 0% -> 0%
where the time goes in v1:
time: 83.2 us; the launch traced here: 82.7 us
  starting transfers between devices  41.1 us (49%)
  waiting for transfers between devices  17.5 us (21%)
  other arithmetic  14.7 us (18%)
  matrix products  6.62 us (8%)
  between operations  1.6 us (2%)
  local copies, waits for them, and re-layouts  1.14 us (1%)
    ppermute x41, starting transfers between devices, exchange(): out.append(lax.ppermute(value, axis, perm))  41.1 us
    ppermute x41, waiting for transfers between devices, exchange(): out.append(lax.ppermute(value, axis, perm))  17.5 us
    reduce_sum x4, other arithmetic, shards(): summed = jnp.sum(jnp.exp(shifted - highest[:, None]), axis=1)  5.41 us
    dot_general x1, matrix products, shards(): scores = jnp.dot(src_all.T, weighted, precision=exact)  3.6 us
    reduce_sum x4, other arithmetic, shards(): sums = jnp.sum(jnp.exp(shifted - highest[None, None, :]), axis=1)  2.29 us
    reduce_max x4, other arithmetic, shards(): highest = jnp.max(shifted, axis=(0, 1))  1.68 us
  transfers between devices with their start and end apart: 41, of which 16 were waited for; matrix products, arithmetic and copies ran while one was open for 4% of the time, Pallas kernels for 0%

profile of v1, /device:TPU:0, one launch (start us, length us, event | category | flops | bytes accessed | tf_op | source)
XLA Modules:
  0.0 82.7 jit_solution(5747025628691215344)
XLA Ops:
  0.6 1.0 %copy-done = bf16[512,512]{1,0:T(8,128)(2,1)S(1)} copy-done((bf16[512,512]{1,0:T(8,128)(2,1)S(1)}, bf16[512,512]{1,0:T(8,128)(2,1)}, u32[]{:S(2)}) %copy-start) | copy-done | bytes 524312
  1.7 1.0 %fusion.19 = f32[50,512]{1,0:T(8,128)S(1)} fusion(bf16[50,512]{1,0:T(8,128)(2,1)} %param.6, bf16[512,512]{1,0:T(8,128)(2,1)S(1)} %copy-done), kind=kOutput, calls=%fused_computation.63 | convolution fusion | flops 26214400 | bytes 677888 | tf_op jit(solution)/shard_map/dot_general | solution.py:74
  2.7 1.0 %fusion.20 = f32[50,50]{1,0:T(8,128)S(1)} fusion(f32[50,512]{1,0:T(8,128)S(1)} %fusion.19, bf16[50,512]{1,0:T(8,128)(2,1)} %param.7), kind=kOutput, calls=%fused_computation.64 | convolution fusion | flops 15360000 | bytes 163600 | tf_op jit(solution)/shard_map/dot_general | solution.py:75
  3.7 3.4 %collective-permute-start.9 = (f32[50,50]{1,0:T(8,128)S(1)}, f32[50,50]{1,0:T(8,128)S(1)}, u32[]{:S(2)}, u32[]{:S(2)}) collective-permute-start(f32[50,50]{1,0:T(8,128)S(1)} %fusion.20), channel_id=1, source_target_pairs={{0,7},{1,6},{2,5},{3,4},{4,3},{5,2},{6,1},{7,0},{8,15},{9,14},{10,... | collective-permute-start | bytes 30008 | tf_op jit(solution)/shard_map/ppermute | solution.py:24
  7.7 1.4 %collective-permute-start.7 = (f32[50,50]{1,0:T(8,128)S(1)}, f32[50,50]{1,0:T(8,128)S(1)}, u32[]{:S(2)}, u32[]{:S(2)}) collective-permute-start(f32[50,50]{1,0:T(8,128)S(1)} %fusion.20), channel_id=1, source_target_pairs={{0,5},{1,4},{2,7},{3,6},{4,1},{5,0},{6,3},{7,2},{8,13},{9,12},{10,... | collective-permute-start | bytes 30008 | tf_op jit(solution)/shard_map/ppermute | solution.py:24
  9.4 1.2 %collective-permute-start.5 = (f32[50,50]{1,0:T(8,128)S(1)}, f32[50,50]{1,0:T(8,128)S(1)}, u32[]{:S(2)}, u32[]{:S(2)}) collective-permute-start(f32[50,50]{1,0:T(8,128)S(1)} %fusion.20), channel_id=1, source_target_pairs={{0,3},{1,2},{2,1},{3,0},{4,7},{5,6},{6,5},{7,4},{8,11},{9,10},{10,... | collective-permute-start | bytes 30008 | tf_op jit(solution)/shard_map/ppermute | solution.py:24
  13.0 1.5 %collective-permute-done.4 = f32[50,50]{1,0:T(8,128)S(1)} collective-permute-done((f32[50,50]{1,0:T(8,128)S(1)}, f32[50,50]{1,0:T(8,128)S(1)}, u32[]{:S(2)}, u32[]{:S(2)}) %collective-permute-start.4) | collective-permute-done | bytes 10032 | tf_op jit(solution)/shard_map/ppermute | solution.py:24
  14.5 3.7 %collective-permute-start.12 = (f32[50,50]{1,0:T(8,128)S(1)}, f32[50,50]{1,0:T(8,128)S(1)}, u32[]{:S(2)}, u32[]{:S(2)}) collective-permute-start(f32[50,50]{1,0:T(8,128)S(1)} %add_add_fusion), channel_id=1, source_target_pairs={{0,24},{8,16},{16,8},{24,0},{1,25},{9,17},{17,9},{25,1},{2,26},{10... | collective-permute-start | bytes 30008 | tf_op jit(solution)/shard_map/ppermute | solution.py:24
  19.6 3.7 %collective-permute-start.2 = (f32[51,512]{1,0:T(8,128)S(1)}, f32[51,512]{1,0:T(8,128)S(1)}, u32[]{:S(2)}, u32[]{:S(2)}) collective-permute-start(f32[51,512]{1,0:T(8,128)S(1)} %pad_maximum_fusion.1), channel_id=1, source_target_pairs={{0,24},{8,16},{16,8},{24,0},{1,25},{9,17},{17,9},{25,1},{2,26},{10... | collective-permute-start | bytes 313352 | tf_op jit(solution)/shard_map/ppermute | solution.py:24
  25.4 1.0 %convolution_multiply_fusion = f32[50,512]{1,0:T(8,128)S(1)} fusion(bf16[50,512]{1,0:T(8,128)(2,1)} %param.7, f32[50,50]{1,0:T(8,128)S(1)} %get-tuple-element.12, f32[]{:T(128)S(6)} %sqrt.3), kind=kOutput, calls=%fused_computation.15 | convolution fusion | flops 15388100 | bytes 163604 | tf_op jit(solution)/shard_map/dot_general | solution.py:79
  26.4 1.2 %collective-permute-done.2 = f32[51,512]{1,0:T(8,128)S(1)} collective-permute-done((f32[51,512]{1,0:T(8,128)S(1)}, f32[51,512]{1,0:T(8,128)S(1)}, u32[]{:S(2)}, u32[]{:S(2)}) %collective-permute-start.2) | collective-permute-done | bytes 104480 | tf_op jit(solution)/shard_map/ppermute | solution.py:24
  27.6 4.8 %collective-permute-done.1 = f32[51,512]{1,0:T(8,128)S(1)} collective-permute-done((f32[51,512]{1,0:T(8,128)S(1)}, f32[51,512]{1,0:T(8,128)S(1)}, u32[]{:S(2)}, u32[]{:S(2)}) %collective-permute-start.1) | collective-permute-done | bytes 104480 | tf_op jit(solution)/shard_map/ppermute | solution.py:24
  33.1 3.6 %fusion.18 = (f32[2048]{0:T(1024)S(1)}, f32[2048,512]{1,0:T(8,128)S(1)}) fusion(f32[50,512]{1,0:T(8,128)S(1)} %convolution_multiply_fusion, f32[51,2048]{1,0:T(8,128)S(1)} %pad_maximum_fusion), kind=kOutput, calls=%fused_computation.62 | convolution fusion | flops 630192128 | bytes 4722688 | tf_op jit(solution)/shard_map/dot_general | solution.py:84
  36.7 1.6 %exponential_reduce_fusion.7 = f32[2048]{0:T(1024)S(1)} fusion(f32[2048,512]{1,0:T(8,128)S(1)} %get-tuple-element.14, f32[2048]{0:T(1024)S(1)} %get-tuple-element.13), kind=kLoop, calls=%fused_computation.7 | loop fusion | flops 2095104 | bytes 4210688 | tf_op jit(solution)/shard_map/reduce_sum | solution.py:91
  38.4 1.0 %collective-permute-start.19 = (f32[2048]{0:T(1024)S(1)}, f32[2048]{0:T(1024)S(1)}, u32[]{:S(2)}, u32[]{:S(2)}) collective-permute-start(f32[2048]{0:T(1024)S(1)} %log_add_fusion.3), channel_id=1, source_target_pairs={{0,7},{1,6},{2,5},{3,4},{4,3},{5,2},{6,1},{7,0},{8,15},{9,14},{10,... | collective-permute-start | bytes 24584 | tf_op jit(solution)/shard_map/ppermute | solution.py:24
  39.4 1.2 %collective-permute-start.18 = (f32[2048]{0:T(1024)S(1)}, f32[2048]{0:T(1024)S(1)}, u32[]{:S(2)}, u32[]{:S(2)}) collective-permute-start(f32[2048]{0:T(1024)S(1)} %log_add_fusion.3), channel_id=1, source_target_pairs={{0,6},{1,7},{2,4},{3,5},{4,2},{5,3},{6,0},{7,1},{8,14},{9,15},{10,... | collective-permute-start | bytes 24584 | tf_op jit(solution)/shard_map/ppermute | solution.py:24
  40.6 1.7 %collective-permute-start.17 = (f32[2048]{0:T(1024)S(1)}, f32[2048]{0:T(1024)S(1)}, u32[]{:S(2)}, u32[]{:S(2)}) collective-permute-start(f32[2048]{0:T(1024)S(1)} %log_add_fusion.3), channel_id=1, source_target_pairs={{0,5},{1,4},{2,7},{3,6},{4,1},{5,0},{6,3},{7,2},{8,13},{9,12},{10,... | collective-permute-start | bytes 24584 | tf_op jit(solution)/shard_map/ppermute | solution.py:24
  44.8 1.2 %collective-permute-done.16 = f32[2048]{0:T(1024)S(1)} collective-permute-done((f32[2048]{0:T(1024)S(1)}, f32[2048]{0:T(1024)S(1)}, u32[]{:S(2)}, u32[]{:S(2)}) %collective-permute-start.16) | collective-permute-done | bytes 8224 | tf_op jit(solution)/shard_map/ppermute | solution.py:24
  48.4 1.2 %exponential_reduce_fusion.5 = f32[2048]{0:T(1024)S(1)} fusion(f32[2048,512]{1,0:T(8,128)S(1)} %get-tuple-element.14, f32[2048]{0:T(1024)S(1)} %add_reduce_fusion.2, f32[512]{0:T(512)S(1)} %subtract_multiply_fusion.7), kind=kLoop, calls=%fused_computation.5 | loop fusion | flops 3143680 | bytes 4212736 | tf_op jit(solution)/shard_map/reduce_sum | solution.py:91
  49.6 1.6 %collective-permute-start.26 = (f32[2048]{0:T(1024)S(1)}, f32[2048]{0:T(1024)S(1)}, u32[]{:S(2)}, u32[]{:S(2)}) collective-permute-start(f32[2048]{0:T(1024)S(1)} %log_add_fusion.2), channel_id=1, source_target_pairs={{0,7},{1,6},{2,5},{3,4},{4,3},{5,2},{6,1},{7,0},{8,15},{9,14},{10,... | collective-permute-start | bytes 24584 | tf_op jit(solution)/shard_map/ppermute | solution.py:24
  51.9 1.4 %collective-permute-start.24 = (f32[2048]{0:T(1024)S(1)}, f32[2048]{0:T(1024)S(1)}, u32[]{:S(2)}, u32[]{:S(2)}) collective-permute-start(f32[2048]{0:T(1024)S(1)} %log_add_fusion.2), channel_id=1, source_target_pairs={{0,5},{1,4},{2,7},{3,6},{4,1},{5,0},{6,3},{7,2},{8,13},{9,12},{10,... | collective-permute-start | bytes 24584 | tf_op jit(solution)/shard_map/ppermute | solution.py:24
  59.5 1.4 %exponential_reduce_fusion.3 = f32[2048]{0:T(1024)S(1)} fusion(f32[2048,512]{1,0:T(8,128)S(1)} %get-tuple-element.14, f32[2048]{0:T(1024)S(1)} %add_reduce_fusion.1, f32[512]{0:T(512)S(1)} %subtract_multiply_fusion.6), kind=kLoop, calls=%fused_computation.3 | loop fusion | flops 3143680 | bytes 4212736 | tf_op jit(solution)/shard_map/reduce_sum | solution.py:91
  61.9 1.2 %collective-permute-start.32 = (f32[2048]{0:T(1024)S(1)}, f32[2048]{0:T(1024)S(1)}, u32[]{:S(2)}, u32[]{:S(2)}) collective-permute-start(f32[2048]{0:T(1024)S(1)} %log_add_fusion.1), channel_id=1, source_target_pairs={{0,6},{1,7},{2,4},{3,5},{4,2},{5,3},{6,0},{7,1},{8,14},{9,15},{10,... | collective-permute-start | bytes 24584 | tf_op jit(solution)/shard_map/ppermute | solution.py:24
  63.1 2.0 %collective-permute-start.31 = (f32[2048]{0:T(1024)S(1)}, f32[2048]{0:T(1024)S(1)}, u32[]{:S(2)}, u32[]{:S(2)}) collective-permute-start(f32[2048]{0:T(1024)S(1)} %log_add_fusion.1), channel_id=1, source_target_pairs={{0,5},{1,4},{2,7},{3,6},{4,1},{5,0},{6,3},{7,2},{8,13},{9,12},{10,... | collective-permute-start | bytes 24584 | tf_op jit(solution)/shard_map/ppermute | solution.py:24
  65.7 1.1 %collective-permute-start.28 = (f32[2048]{0:T(1024)S(1)}, f32[2048]{0:T(1024)S(1)}, u32[]{:S(2)}, u32[]{:S(2)}) collective-permute-start(f32[2048]{0:T(1024)S(1)} %log_add_fusion.1), channel_id=1, source_target_pairs={{0,2},{1,3},{2,0},{3,1},{4,6},{5,7},{6,4},{7,5},{8,10},{9,11},{10,... | collective-permute-start | bytes 24584 | tf_op jit(solution)/shard_map/ppermute | solution.py:24
  67.2 1.5 %collective-permute-done.30 = f32[2048]{0:T(1024)S(1)} collective-permute-done((f32[2048]{0:T(1024)S(1)}, f32[2048]{0:T(1024)S(1)}, u32[]{:S(2)}, u32[]{:S(2)}) %collective-permute-start.30) | collective-permute-done | bytes 8224 | tf_op jit(solution)/shard_map/ppermute | solution.py:24
  70.8 1.2 %exponential_reduce_fusion.1 = f32[2048]{0:T(1024)S(1)} fusion(f32[2048,512]{1,0:T(8,128)S(1)} %get-tuple-element.14, f32[2048]{0:T(1024)S(1)} %add_reduce_fusion, f32[512]{0:T(512)S(1)} %subtract_multiply_fusion.5), kind=kLoop, calls=%fused_computation.1 | loop fusion | flops 3143680 | bytes 4212736 | tf_op jit(solution)/shard_map/reduce_sum | solution.py:91
  72.0 1.5 %collective-permute-start.40 = (f32[2048]{0:T(1024)S(1)}, f32[2048]{0:T(1024)S(1)}, u32[]{:S(2)}, u32[]{:S(2)}) collective-permute-start(f32[2048]{0:T(1024)S(1)} %log_add_fusion), channel_id=1, source_target_pairs={{0,7},{1,6},{2,5},{3,4},{4,3},{5,2},{6,1},{7,0},{8,15},{9,14},{10,... | collective-permute-start | bytes 24584 | tf_op jit(solution)/shard_map/ppermute | solution.py:24
  74.2 1.7 %collective-permute-start.38 = (f32[2048]{0:T(1024)S(1)}, f32[2048]{0:T(1024)S(1)}, u32[]{:S(2)}, u32[]{:S(2)}) collective-permute-start(f32[2048]{0:T(1024)S(1)} %log_add_fusion), channel_id=1, source_target_pairs={{0,5},{1,4},{2,7},{3,6},{4,1},{5,0},{6,3},{7,2},{8,13},{9,12},{10,... | collective-permute-start | bytes 24584 | tf_op jit(solution)/shard_map/ppermute | solution.py:24
  76.8 1.1 %collective-permute-start.35 = (f32[2048]{0:T(1024)S(1)}, f32[2048]{0:T(1024)S(1)}, u32[]{:S(2)}, u32[]{:S(2)}) collective-permute-start(f32[2048]{0:T(1024)S(1)} %log_add_fusion), channel_id=1, source_target_pairs={{0,2},{1,3},{2,0},{3,1},{4,6},{5,7},{6,4},{7,5},{8,10},{9,11},{10,... | collective-permute-start | bytes 24584 | tf_op jit(solution)/shard_map/ppermute | solution.py:24
  78.3 1.2 %collective-permute-done.37 = f32[2048]{0:T(1024)S(1)} collective-permute-done((f32[2048]{0:T(1024)S(1)}, f32[2048]{0:T(1024)S(1)}, u32[]{:S(2)}, u32[]{:S(2)}) %collective-permute-start.37) | collective-permute-done | bytes 8224 | tf_op jit(solution)/shard_map/ppermute | solution.py:24
  81.6 1.1 %fusion = f32[512,512]{1,0:T(8,128)} fusion(f32[2048,512]{1,0:T(8,128)S(1)} %get-tuple-element.14, f32[512]{0:T(512)S(1)} %subtract_multiply_fusion.4, f32[512]{0:T(512)S(1)} %slice.94), kind=kLoop, calls=%fused_computation.17 | loop fusion | flops 524288 | bytes 2101248 | tf_op jit(solution)/shard_map/add | solution.py:99
  (103 shorter events, 26.6 us)
Async XLA Ops:
  3.7 6.9 %collective-permute-start.9 = (f32[50,50]{1,0:T(8,128)S(1)}, f32[50,50]{1,0:T(8,128)S(1)}, u32[]{:S(2)}, u32[]{:S(2)}) collective-permute-start(f32[50,50]{1,0:T(8,128)S(1)} %fusion.20), channel_id=1, source_target_pairs={{0,7},{1,6},{2,5},{3,4},{4,3},{5,2},{6,1},{7,0},{8,15},{9,14},{10,... | collective-permute-start | bytes 30008 | tf_op jit(solution)/shard_map/ppermute | solution.py:24
  7.1 4.9 %collective-permute-start.8 = (f32[50,50]{1,0:T(8,128)S(1)}, f32[50,50]{1,0:T(8,128)S(1)}, u32[]{:S(2)}, u32[]{:S(2)}) collective-permute-start(f32[50,50]{1,0:T(8,128)S(1)} %fusion.20), channel_id=1, source_target_pairs={{0,6},{1,7},{2,4},{3,5},{4,2},{5,3},{6,0},{7,1},{8,14},{9,15},{10,... | collective-permute-start | bytes 30008 | tf_op jit(solution)/shard_map/ppermute | solution.py:24
  7.7 5.1 %collective-permute-start.7 = (f32[50,50]{1,0:T(8,128)S(1)}, f32[50,50]{1,0:T(8,128)S(1)}, u32[]{:S(2)}, u32[]{:S(2)}) collective-permute-start(f32[50,50]{1,0:T(8,128)S(1)} %fusion.20), channel_id=1, source_target_pairs={{0,5},{1,4},{2,7},{3,6},{4,1},{5,0},{6,3},{7,2},{8,13},{9,12},{10,... | collective-permute-start | bytes 30008 | tf_op jit(solution)/shard_map/ppermute | solution.py:24
  9.1 3.9 %collective-permute-start.6 = (f32[50,50]{1,0:T(8,128)S(1)}, f32[50,50]{1,0:T(8,128)S(1)}, u32[]{:S(2)}, u32[]{:S(2)}) collective-permute-start(f32[50,50]{1,0:T(8,128)S(1)} %fusion.20), channel_id=1, source_target_pairs={{0,4},{1,5},{2,6},{3,7},{4,0},{5,1},{6,2},{7,3},{8,12},{9,13},{10,... | collective-permute-start | bytes 30008 | tf_op jit(solution)/shard_map/ppermute | solution.py:24
  9.4 3.6 %collective-permute-start.5 = (f32[50,50]{1,0:T(8,128)S(1)}, f32[50,50]{1,0:T(8,128)S(1)}, u32[]{:S(2)}, u32[]{:S(2)}) collective-permute-start(f32[50,50]{1,0:T(8,128)S(1)} %fusion.20), channel_id=1, source_target_pairs={{0,3},{1,2},{2,1},{3,0},{4,7},{5,6},{6,5},{7,4},{8,11},{9,10},{10,... | collective-permute-start | bytes 30008 | tf_op jit(solution)/shard_map/ppermute | solution.py:24
  10.6 3.9 %collective-permute-start.4 = (f32[50,50]{1,0:T(8,128)S(1)}, f32[50,50]{1,0:T(8,128)S(1)}, u32[]{:S(2)}, u32[]{:S(2)}) collective-permute-start(f32[50,50]{1,0:T(8,128)S(1)} %fusion.20), channel_id=1, source_target_pairs={{0,2},{1,3},{2,0},{3,1},{4,6},{5,7},{6,4},{7,5},{8,10},{9,11},{10,... | collective-permute-start | bytes 30008 | tf_op jit(solution)/shard_map/ppermute | solution.py:24
  14.5 8.8 %collective-permute-start.12 = (f32[50,50]{1,0:T(8,128)S(1)}, f32[50,50]{1,0:T(8,128)S(1)}, u32[]{:S(2)}, u32[]{:S(2)}) collective-permute-start(f32[50,50]{1,0:T(8,128)S(1)} %add_add_fusion), channel_id=1, source_target_pairs={{0,24},{8,16},{16,8},{24,0},{1,25},{9,17},{17,9},{25,1},{2,26},{10... | collective-permute-start | bytes 30008 | tf_op jit(solution)/shard_map/ppermute | solution.py:24
  18.2 5.9 %collective-permute-start.11 = (f32[50,50]{1,0:T(8,128)S(1)}, f32[50,50]{1,0:T(8,128)S(1)}, u32[]{:S(2)}, u32[]{:S(2)}) collective-permute-start(f32[50,50]{1,0:T(8,128)S(1)} %add_add_fusion), channel_id=1, source_target_pairs={{0,16},{8,24},{16,0},{24,8},{1,17},{9,25},{17,1},{25,9},{2,18},{10... | collective-permute-start | bytes 30008 | tf_op jit(solution)/shard_map/ppermute | solution.py:24
  18.2 5.9 %collective-permute-start.10 = (f32[50,50]{1,0:T(8,128)S(1)}, f32[50,50]{1,0:T(8,128)S(1)}, u32[]{:S(2)}, u32[]{:S(2)}) collective-permute-start(f32[50,50]{1,0:T(8,128)S(1)} %add_add_fusion), channel_id=1, source_target_pairs={{0,8},{8,0},{16,24},{24,16},{1,9},{9,1},{17,25},{25,17},{2,10},{10... | collective-permute-start | bytes 30008 | tf_op jit(solution)/shard_map/ppermute | solution.py:24
  19.6 7.9 %collective-permute-start.2 = (f32[51,512]{1,0:T(8,128)S(1)}, f32[51,512]{1,0:T(8,128)S(1)}, u32[]{:S(2)}, u32[]{:S(2)}) collective-permute-start(f32[51,512]{1,0:T(8,128)S(1)} %pad_maximum_fusion.1), channel_id=1, source_target_pairs={{0,24},{8,16},{16,8},{24,0},{1,25},{9,17},{17,9},{25,1},{2,26},{10... | collective-permute-start | bytes 313352 | tf_op jit(solution)/shard_map/ppermute | solution.py:24
  23.3 9.1 %collective-permute-start.1 = (f32[51,512]{1,0:T(8,128)S(1)}, f32[51,512]{1,0:T(8,128)S(1)}, u32[]{:S(2)}, u32[]{:S(2)}) collective-permute-start(f32[51,512]{1,0:T(8,128)S(1)} %pad_maximum_fusion.1), channel_id=1, source_target_pairs={{0,16},{8,24},{16,0},{24,8},{1,17},{9,25},{17,1},{25,9},{2,18},{10... | collective-permute-start | bytes 313352 | tf_op jit(solution)/shard_map/ppermute | solution.py:24
  23.3 9.1 %collective-permute-start = (f32[51,512]{1,0:T(8,128)S(1)}, f32[51,512]{1,0:T(8,128)S(1)}, u32[]{:S(2)}, u32[]{:S(2)}) collective-permute-start(f32[51,512]{1,0:T(8,128)S(1)} %pad_maximum_fusion.1), channel_id=1, source_target_pairs={{0,8},{8,0},{16,24},{24,16},{1,9},{9,1},{17,25},{25,17},{2,10},{10... | collective-permute-start | bytes 313352 | tf_op jit(solution)/shard_map/ppermute | solution.py:24
  38.4 4.8 %collective-permute-start.19 = (f32[2048]{0:T(1024)S(1)}, f32[2048]{0:T(1024)S(1)}, u32[]{:S(2)}, u32[]{:S(2)}) collective-permute-start(f32[2048]{0:T(1024)S(1)} %log_add_fusion.3), channel_id=1, source_target_pairs={{0,7},{1,6},{2,5},{3,4},{4,3},{5,2},{6,1},{7,0},{8,15},{9,14},{10,... | collective-permute-start | bytes 24584 | tf_op jit(solution)/shard_map/ppermute | solution.py:24
  39.4 4.7 %collective-permute-start.18 = (f32[2048]{0:T(1024)S(1)}, f32[2048]{0:T(1024)S(1)}, u32[]{:S(2)}, u32[]{:S(2)}) collective-permute-start(f32[2048]{0:T(1024)S(1)} %log_add_fusion.3), channel_id=1, source_target_pairs={{0,6},{1,7},{2,4},{3,5},{4,2},{5,3},{6,0},{7,1},{8,14},{9,15},{10,... | collective-permute-start | bytes 24584 | tf_op jit(solution)/shard_map/ppermute | solution.py:24
  40.6 4.1 %collective-permute-start.17 = (f32[2048]{0:T(1024)S(1)}, f32[2048]{0:T(1024)S(1)}, u32[]{:S(2)}, u32[]{:S(2)}) collective-permute-start(f32[2048]{0:T(1024)S(1)} %log_add_fusion.3), channel_id=1, source_target_pairs={{0,5},{1,4},{2,7},{3,6},{4,1},{5,0},{6,3},{7,2},{8,13},{9,12},{10,... | collective-permute-start | bytes 24584 | tf_op jit(solution)/shard_map/ppermute | solution.py:24
  42.3 3.7 %collective-permute-start.16 = (f32[2048]{0:T(1024)S(1)}, f32[2048]{0:T(1024)S(1)}, u32[]{:S(2)}, u32[]{:S(2)}) collective-permute-start(f32[2048]{0:T(1024)S(1)} %log_add_fusion.3), channel_id=1, source_target_pairs={{0,4},{1,5},{2,6},{3,7},{4,0},{5,1},{6,2},{7,3},{8,12},{9,13},{10,... | collective-permute-start | bytes 24584 | tf_op jit(solution)/shard_map/ppermute | solution.py:24
  43.2 3.7 %collective-permute-start.14 = (f32[2048]{0:T(1024)S(1)}, f32[2048]{0:T(1024)S(1)}, u32[]{:S(2)}, u32[]{:S(2)}) collective-permute-start(f32[2048]{0:T(1024)S(1)} %log_add_fusion.3), channel_id=1, source_target_pairs={{0,2},{1,3},{2,0},{3,1},{4,6},{5,7},{6,4},{7,5},{8,10},{9,11},{10,... | collective-permute-start | bytes 24584 | tf_op jit(solution)/shard_map/ppermute | solution.py:24
  49.6 4.8 %collective-permute-start.26 = (f32[2048]{0:T(1024)S(1)}, f32[2048]{0:T(1024)S(1)}, u32[]{:S(2)}, u32[]{:S(2)}) collective-permute-start(f32[2048]{0:T(1024)S(1)} %log_add_fusion.2), channel_id=1, source_target_pairs={{0,7},{1,6},{2,5},{3,4},{4,3},{5,2},{6,1},{7,0},{8,15},{9,14},{10,... | collective-permute-start | bytes 24584 | tf_op jit(solution)/shard_map/ppermute | solution.py:24
  51.2 4.6 %collective-permute-start.25 = (f32[2048]{0:T(1024)S(1)}, f32[2048]{0:T(1024)S(1)}, u32[]{:S(2)}, u32[]{:S(2)}) collective-permute-start(f32[2048]{0:T(1024)S(1)} %log_add_fusion.2), channel_id=1, source_target_pairs={{0,6},{1,7},{2,4},{3,5},{4,2},{5,3},{6,0},{7,1},{8,14},{9,15},{10,... | collective-permute-start | bytes 24584 | tf_op jit(solution)/shard_map/ppermute | solution.py:24
  51.9 4.0 %collective-permute-start.24 = (f32[2048]{0:T(1024)S(1)}, f32[2048]{0:T(1024)S(1)}, u32[]{:S(2)}, u32[]{:S(2)}) collective-permute-start(f32[2048]{0:T(1024)S(1)} %log_add_fusion.2), channel_id=1, source_target_pairs={{0,5},{1,4},{2,7},{3,6},{4,1},{5,0},{6,3},{7,2},{8,13},{9,12},{10,... | collective-permute-start | bytes 24584 | tf_op jit(solution)/shard_map/ppermute | solution.py:24
  53.3 3.7 %collective-permute-start.23 = (f32[2048]{0:T(1024)S(1)}, f32[2048]{0:T(1024)S(1)}, u32[]{:S(2)}, u32[]{:S(2)}) collective-permute-start(f32[2048]{0:T(1024)S(1)} %log_add_fusion.2), channel_id=1, source_target_pairs={{0,4},{1,5},{2,6},{3,7},{4,0},{5,1},{6,2},{7,3},{8,12},{9,13},{10,... | collective-permute-start | bytes 24584 | tf_op jit(solution)/shard_map/ppermute | solution.py:24
  54.4 3.7 %collective-permute-start.21 = (f32[2048]{0:T(1024)S(1)}, f32[2048]{0:T(1024)S(1)}, u32[]{:S(2)}, u32[]{:S(2)}) collective-permute-start(f32[2048]{0:T(1024)S(1)} %log_add_fusion.2), channel_id=1, source_target_pairs={{0,2},{1,3},{2,0},{3,1},{4,6},{5,7},{6,4},{7,5},{8,10},{9,11},{10,... | collective-permute-start | bytes 24584 | tf_op jit(solution)/shard_map/ppermute | solution.py:24
  60.9 4.8 %collective-permute-start.33 = (f32[2048]{0:T(1024)S(1)}, f32[2048]{0:T(1024)S(1)}, u32[]{:S(2)}, u32[]{:S(2)}) collective-permute-start(f32[2048]{0:T(1024)S(1)} %log_add_fusion.1), channel_id=1, source_target_pairs={{0,7},{1,6},{2,5},{3,4},{4,3},{5,2},{6,1},{7,0},{8,15},{9,14},{10,... | collective-permute-start | bytes 24584 | tf_op jit(solution)/shard_map/ppermute | solution.py:24
  61.9 5.0 %collective-permute-start.32 = (f32[2048]{0:T(1024)S(1)}, f32[2048]{0:T(1024)S(1)}, u32[]{:S(2)}, u32[]{:S(2)}) collective-permute-start(f32[2048]{0:T(1024)S(1)} %log_add_fusion.1), channel_id=1, source_target_pairs={{0,6},{1,7},{2,4},{3,5},{4,2},{5,3},{6,0},{7,1},{8,14},{9,15},{10,... | collective-permute-start | bytes 24584 | tf_op jit(solution)/shard_map/ppermute | solution.py:24
  63.1 4.2 %collective-permute-start.31 = (f32[2048]{0:T(1024)S(1)}, f32[2048]{0:T(1024)S(1)}, u32[]{:S(2)}, u32[]{:S(2)}) collective-permute-start(f32[2048]{0:T(1024)S(1)} %log_add_fusion.1), channel_id=1, source_target_pairs={{0,5},{1,4},{2,7},{3,6},{4,1},{5,0},{6,3},{7,2},{8,13},{9,12},{10,... | collective-permute-start | bytes 24584 | tf_op jit(solution)/shard_map/ppermute | solution.py:24
  65.1 3.7 %collective-permute-start.30 = (f32[2048]{0:T(1024)S(1)}, f32[2048]{0:T(1024)S(1)}, u32[]{:S(2)}, u32[]{:S(2)}) collective-permute-start(f32[2048]{0:T(1024)S(1)} %log_add_fusion.1), channel_id=1, source_target_pairs={{0,4},{1,5},{2,6},{3,7},{4,0},{5,1},{6,2},{7,3},{8,12},{9,13},{10,... | collective-permute-start | bytes 24584 | tf_op jit(solution)/shard_map/ppermute | solution.py:24
  65.7 3.7 %collective-permute-start.28 = (f32[2048]{0:T(1024)S(1)}, f32[2048]{0:T(1024)S(1)}, u32[]{:S(2)}, u32[]{:S(2)}) collective-permute-start(f32[2048]{0:T(1024)S(1)} %log_add_fusion.1), channel_id=1, source_target_pairs={{0,2},{1,3},{2,0},{3,1},{4,6},{5,7},{6,4},{7,5},{8,10},{9,11},{10,... | collective-permute-start | bytes 24584 | tf_op jit(solution)/shard_map/ppermute | solution.py:24
  72.0 4.7 %collective-permute-start.40 = (f32[2048]{0:T(1024)S(1)}, f32[2048]{0:T(1024)S(1)}, u32[]{:S(2)}, u32[]{:S(2)}) collective-permute-start(f32[2048]{0:T(1024)S(1)} %log_add_fusion), channel_id=1, source_target_pairs={{0,7},{1,6},{2,5},{3,4},{4,3},{5,2},{6,1},{7,0},{8,15},{9,14},{10,... | collective-permute-start | bytes 24584 | tf_op jit(solution)/shard_map/ppermute | solution.py:24
  73.5 4.6 %collective-permute-start.39 = (f32[2048]{0:T(1024)S(1)}, f32[2048]{0:T(1024)S(1)}, u32[]{:S(2)}, u32[]{:S(2)}) collective-permute-start(f32[2048]{0:T(1024)S(1)} %log_add_fusion), channel_id=1, source_target_pairs={{0,6},{1,7},{2,4},{3,5},{4,2},{5,3},{6,0},{7,1},{8,14},{9,15},{10,... | collective-permute-start | bytes 24584 | tf_op jit(solution)/shard_map/ppermute | solution.py:24
  74.2 4.1 %collective-permute-start.38 = (f32[2048]{0:T(1024)S(1)}, f32[2048]{0:T(1024)S(1)}, u32[]{:S(2)}, u32[]{:S(2)}) collective-permute-start(f32[2048]{0:T(1024)S(1)} %log_add_fusion), channel_id=1, source_target_pairs={{0,5},{1,4},{2,7},{3,6},{4,1},{5,0},{6,3},{7,2},{8,13},{9,12},{10,... | collective-permute-start | bytes 24584 | tf_op jit(solution)/shard_map/ppermute | solution.py:24
  75.9 3.7 %collective-permute-start.37 = (f32[2048]{0:T(1024)S(1)}, f32[2048]{0:T(1024)S(1)}, u32[]{:S(2)}, u32[]{:S(2)}) collective-permute-start(f32[2048]{0:T(1024)S(1)} %log_add_fusion), channel_id=1, source_target_pairs={{0,4},{1,5},{2,6},{3,7},{4,0},{5,1},{6,2},{7,3},{8,12},{9,13},{10,... | collective-permute-start | bytes 24584 | tf_op jit(solution)/shard_map/ppermute | solution.py:24
  76.8 3.7 %collective-permute-start.35 = (f32[2048]{0:T(1024)S(1)}, f32[2048]{0:T(1024)S(1)}, u32[]{:S(2)}, u32[]{:S(2)}) collective-permute-start(f32[2048]{0:T(1024)S(1)} %log_add_fusion), channel_id=1, source_target_pairs={{0,2},{1,3},{2,0},{3,1},{4,6},{5,7},{6,4},{7,5},{8,10},{9,11},{10,... | collective-permute-start | bytes 24584 | tf_op jit(solution)/shard_map/ppermute | solution.py:24
  (14 other events, 40.7 us)

commit v2 on v1

--- a/solution.py
+++ b/solution.py
@@ -13,7 +13,7 @@
 marg_power = 1.0 / (1.0 + eps_reg)
 tiny_eps = 1e-06
 
-RADIX = 8
+RADIX = 2
 
 
 def exchange(value, axis, low, span):
@@ -57,9 +57,9 @@
 
 def all_blocks(value, axis):
     blocks = [value]
-    for low, span in stages(axis):
-        fresh = [exchange(block, axis, low, span) for block in blocks]
-        blocks = [fresh[b][j] for j in range(span) for b in range(len(blocks))]
+    for j in range(1, lax.axis_size(axis)):
+        perm = [(i, i ^ j) for i in range(lax.axis_size(axis))]
+        blocks.append(lax.ppermute(value, axis, perm))
     return blocks
 
 
@@ -70,20 +70,29 @@
     src_float = src_pcs.astype(jnp.float32)
     tgt_float = tgt_pcs.astype(jnp.float32)
     packed = jnp.concatenate([src_float, src_mass[None, :]], axis=0)
-    src_blocks = all_blocks(packed, "src")
+    half = packed.shape[1] // 2
+    odd = lax.axis_index("tgt") % 2
+    mine = lax.dynamic_slice_in_dim(packed, odd * half, half, axis=1)
+    near = jnp.concatenate(all_blocks(mine, "src"), axis=0)
+    far = lax.ppermute(near, "tgt", [(i, i ^ 1) for i in range(lax.axis_size("tgt"))])
     block_panel = jnp.dot(src_pcs, coupling, preferred_element_type=jnp.float32)
     block_moment = jnp.dot(block_panel, tgt_float.T, precision=exact)
-    moment = all_sum(all_sum(block_moment, "tgt"), "src")
+    moment = all_sum(block_moment, "tgt")
+    moment, near, far = lax.optimization_barrier((moment, near, far))
+    moment = all_sum(moment, "src")
     moment = moment * (total_rows * total_cols) ** (-0.5)
     normed = moment / jnp.sqrt(jnp.mean(moment * moment) + tiny_eps)
     weighted = jnp.dot(normed, tgt_float, precision=exact) * (2.0 / (eps_reg * PCS))
-    everything = jnp.concatenate(src_blocks, axis=1)
+    left = jnp.where(odd == 0, near, far)
+    right = jnp.where(odd == 0, far, near)
+    blocks = lax.axis_size("src")
+    both = jnp.concatenate([left, right], axis=1).reshape(blocks, PCS + 1, -1)
+    everything = jnp.concatenate([both[b] for b in range(blocks)], axis=1)
     src_all = everything[:PCS]
     log_src = jnp.log(everything[PCS]) + jnp.log(jnp.float32(total_cols))
     log_tgt = jnp.log(tgt_mass) + jnp.log(jnp.float32(total_rows))
     scores = jnp.dot(src_all.T, weighted, precision=exact)
     col_potential = jnp.zeros((coupling.shape[1],), jnp.float32)
-    blocks = len(src_blocks)
     rows = coupling.shape[0]
     for iteration in range(ITERS):
         shifted = scores + col_potential[None, :]

time: 83.2 us -> 83.7 us (level)
  waiting for transfers between devices: 17.5 us -> 35.9 us
  starting transfers between devices: 41.1 us -> 25.8 us
  local copies, waits for them, and re-layouts: 1.14 us -> 0.11 us
    ppermute x41 -> x17, starting transfers between devices: 41.1 us -> 20.1 us  [exchange(): out.append(lax.ppermute(value, axis, perm))]
    ppermute x41 -> x17, waiting for transfers between devices: 17.5 us -> 32.5 us  [exchange(): out.append(lax.ppermute(value, axis, perm))]
    ppermute x0 -> x4, starting transfers between devices: none -> 5.76 us  [the longest x3 5.69 us: all_blocks(): blocks.append(lax.ppermute(value, axis, perm))]
    ppermute x0 -> x4, waiting for transfers between devices: none -> 3.41 us  [the longest x3 3.41 us: all_blocks(): blocks.append(lax.ppermute(value, axis, perm))]
    unnamed x10, local copies, waits for them, and re-layouts: 1.14 us -> 0.11 us
  transfers between devices with their start and end apart: 41 -> 21, of which waited for: 16 -> 19; matrix products, arithmetic and copies ran while one was open for 4% -> 3% of each run, Pallas kernels for 0% -> 0%
where the time goes in v2:
time: 83.7 us; the launch traced here: 83.4 us
  waiting for transfers between devices  35.9 us (43%)
  starting transfers between devices  25.8 us (31%)
  other arithmetic  14.1 us (17%)
  matrix products  5.8 us (7%)
  between operations  1.66 us (2%)
    ppermute x17, waiting for transfers between devices, exchange(): out.append(lax.ppermute(value, axis, perm))  32.5 us
    ppermute x17, starting transfers between devices, exchange(): out.append(lax.ppermute(value, axis, perm))  20.1 us
    ppermute x3, starting transfers between devices, all_blocks(): blocks.append(lax.ppermute(value, axis, perm))  5.69 us
    reduce_sum x4, other arithmetic, shards(): summed = jnp.sum(jnp.exp(shifted - highest[:, None]), axis=1)  5.21 us
    dot_general x1, matrix products, shards(): scores = jnp.dot(src_all.T, weighted, precision=exact)  3.6 us
    ppermute x3, waiting for transfers between devices, all_blocks(): blocks.append(lax.ppermute(value, axis, perm))  3.41 us
    reduce_sum x4, other arithmetic, shards(): sums = jnp.sum(jnp.exp(shifted - highest[None, None, :]), axis=1)  2.29 us
    reduce_max x4, other arithmetic, shards(): highest = jnp.max(shifted, axis=(0, 1))  1.7 us
  transfers between devices with their start and end apart: 21, of which 19 were waited for; matrix products, arithmetic and copies ran while one was open for 3% of the time, Pallas kernels for 0%

profile of v2, /device:TPU:0, one launch (start us, length us, event | category | flops | bytes accessed | tf_op | source)
XLA Modules:
  0.0 83.4 jit_solution(16874907185762580624)
XLA Ops:
  2.3 5.1 %collective-permute-start.5 = (f32[51,256]{1,0:T(8,128)S(1)}, f32[51,256]{1,0:T(8,128)S(1)}, u32[]{:S(2)}, u32[]{:S(2)}) collective-permute-start(f32[51,256]{1,0:T(8,128)S(1)} %fusion.7), channel_id=1, source_target_pairs={{0,24},{8,16},{16,8},{24,0},{1,25},{9,17},{17,9},{25,1},{2,26},{10... | collective-permute-start | bytes 156680 | tf_op jit(solution)/shard_map/ppermute | solution.py:62
  9.8 2.7 %collective-permute-done.4 = f32[51,256]{1,0:T(8,128)S(1)} collective-permute-done((f32[51,256]{1,0:T(8,128)S(1)}, f32[51,256]{1,0:T(8,128)S(1)}, u32[]{:S(2)}, u32[]{:S(2)}) %collective-permute-start.4) | collective-permute-done | bytes 52256 | tf_op jit(solution)/shard_map/ppermute | solution.py:62
  15.0 1.5 %collective-permute-start.1 = (f32[50,50]{1,0:T(8,128)S(1)}, f32[50,50]{1,0:T(8,128)S(1)}, u32[]{:S(2)}, u32[]{:S(2)}) collective-permute-start(f32[50,50]{1,0:T(8,128)S(1)} %add.257), channel_id=1, source_target_pairs={{0,2},{1,3},{2,0},{3,1},{4,6},{5,7},{6,4},{7,5},{8,10},{9,11},{10,... | collective-permute-start | bytes 30008 | tf_op jit(solution)/shard_map/ppermute | solution.py:24
  16.5 2.4 %collective-permute-done.1 = f32[50,50]{1,0:T(8,128)S(1)} collective-permute-done((f32[50,50]{1,0:T(8,128)S(1)}, f32[50,50]{1,0:T(8,128)S(1)}, u32[]{:S(2)}, u32[]{:S(2)}) %collective-permute-start.1) | collective-permute-done | bytes 10032 | tf_op jit(solution)/shard_map/ppermute | solution.py:24
  18.9 1.5 %collective-permute-start.2 = (f32[50,50]{1,0:T(8,128)S(1)}, f32[50,50]{1,0:T(8,128)S(1)}, u32[]{:S(2)}, u32[]{:S(2)}) collective-permute-start(f32[50,50]{1,0:T(8,128)S(1)} %add.258), channel_id=1, source_target_pairs={{0,4},{1,5},{2,6},{3,7},{4,0},{5,1},{6,2},{7,3},{8,12},{9,13},{10,... | collective-permute-start | bytes 30008 | tf_op jit(solution)/shard_map/ppermute | solution.py:24
  20.4 2.3 %collective-permute-done.2 = f32[50,50]{1,0:T(8,128)S(1)} collective-permute-done((f32[50,50]{1,0:T(8,128)S(1)}, f32[50,50]{1,0:T(8,128)S(1)}, u32[]{:S(2)}, u32[]{:S(2)}) %collective-permute-start.2) | collective-permute-done | bytes 10032 | tf_op jit(solution)/shard_map/ppermute | solution.py:24
  24.0 2.7 %collective-permute-done.7 = f32[50,50]{1,0:T(8,128)S(1)} collective-permute-done((f32[50,50]{1,0:T(8,128)S(1)}, f32[50,50]{1,0:T(8,128)S(1)}, u32[]{:S(2)}, u32[]{:S(2)}) %collective-permute-start.7) | collective-permute-done | bytes 10032 | tf_op jit(solution)/shard_map/ppermute | solution.py:24
  26.7 2.1 %collective-permute-start.8 = (f32[50,50]{1,0:T(8,128)S(1)}, f32[50,50]{1,0:T(8,128)S(1)}, u32[]{:S(2)}, u32[]{:S(2)}) collective-permute-start(f32[50,50]{1,0:T(8,128)S(1)} %add.261), channel_id=1, source_target_pairs={{0,16},{8,24},{16,0},{24,8},{1,17},{9,25},{17,1},{25,9},{2,18},{10... | collective-permute-start | bytes 30008 | tf_op jit(solution)/shard_map/ppermute | solution.py:24
  28.8 2.6 %collective-permute-done.8 = f32[50,50]{1,0:T(8,128)S(1)} collective-permute-done((f32[50,50]{1,0:T(8,128)S(1)}, f32[50,50]{1,0:T(8,128)S(1)}, u32[]{:S(2)}, u32[]{:S(2)}) %collective-permute-start.8) | collective-permute-done | bytes 10032 | tf_op jit(solution)/shard_map/ppermute | solution.py:24
  33.0 3.6 %fusion.36 = (f32[2048]{0:T(1024)S(1)}, f32[2048,512]{1,0:T(8,128)S(1)}) fusion(f32[50,512]{1,0:T(8,128)S(1)} %convolution_multiply_fusion, f32[51,2048]{1,0:T(8,128)S(1)} %fusion.3), kind=kOutput, calls=%fused_computation.109 | convolution fusion | flops 630192128 | bytes 4722688 | tf_op jit(solution)/shard_map/dot_general | solution.py:94
  36.6 1.6 %exponential_reduce_fusion.7 = f32[2048]{0:T(1024)S(1)} fusion(f32[2048,512]{1,0:T(8,128)S(1)} %get-tuple-element.23, f32[2048]{0:T(1024)S(1)} %get-tuple-element.22), kind=kLoop, calls=%fused_computation.7 | loop fusion | flops 2095104 | bytes 4210688 | tf_op jit(solution)/shard_map/reduce_sum | solution.py:100
  39.5 1.6 %collective-permute-start.10 = (f32[2048]{0:T(1024)S(1)}, f32[2048]{0:T(1024)S(1)}, u32[]{:S(2)}, u32[]{:S(2)}) collective-permute-start(f32[2048]{0:T(1024)S(1)} %log_add_fusion.10), channel_id=1, source_target_pairs={{0,2},{1,3},{2,0},{3,1},{4,6},{5,7},{6,4},{7,5},{8,10},{9,11},{10,... | collective-permute-start | bytes 24584 | tf_op jit(solution)/shard_map/ppermute | solution.py:24
  41.1 2.1 %collective-permute-done.10 = f32[2048]{0:T(1024)S(1)} collective-permute-done((f32[2048]{0:T(1024)S(1)}, f32[2048]{0:T(1024)S(1)}, u32[]{:S(2)}, u32[]{:S(2)}) %collective-permute-start.10) | collective-permute-done | bytes 8224 | tf_op jit(solution)/shard_map/ppermute | solution.py:24
  43.2 1.6 %collective-permute-start.11 = (f32[2048]{0:T(1024)S(1)}, f32[2048]{0:T(1024)S(1)}, u32[]{:S(2)}, u32[]{:S(2)}) collective-permute-start(f32[2048]{0:T(1024)S(1)} %log_add_fusion.9), channel_id=1, source_target_pairs={{0,4},{1,5},{2,6},{3,7},{4,0},{5,1},{6,2},{7,3},{8,12},{9,13},{10,... | collective-permute-start | bytes 24584 | tf_op jit(solution)/shard_map/ppermute | solution.py:24
  44.8 2.1 %collective-permute-done.11 = f32[2048]{0:T(1024)S(1)} collective-permute-done((f32[2048]{0:T(1024)S(1)}, f32[2048]{0:T(1024)S(1)}, u32[]{:S(2)}, u32[]{:S(2)}) %collective-permute-start.11) | collective-permute-done | bytes 8224 | tf_op jit(solution)/shard_map/ppermute | solution.py:24
  48.4 1.2 %exponential_reduce_fusion.5 = f32[2048]{0:T(1024)S(1)} fusion(f32[2048,512]{1,0:T(8,128)S(1)} %get-tuple-element.23, f32[2048]{0:T(1024)S(1)} %add_reduce_fusion.2, f32[512]{0:T(512)S(1)} %subtract_multiply_fusion.7), kind=kLoop, calls=%fused_computation.5 | loop fusion | flops 3143680 | bytes 4212736 | tf_op jit(solution)/shard_map/reduce_sum | solution.py:100
  49.7 1.2 %collective-permute-done.12 = f32[2048]{0:T(1024)S(1)} collective-permute-done((f32[2048]{0:T(1024)S(1)}, f32[2048]{0:T(1024)S(1)}, u32[]{:S(2)}, u32[]{:S(2)}) %collective-permute-start.12) | collective-permute-done | bytes 8224 | tf_op jit(solution)/shard_map/ppermute | solution.py:24
  50.9 1.6 %collective-permute-start.13 = (f32[2048]{0:T(1024)S(1)}, f32[2048]{0:T(1024)S(1)}, u32[]{:S(2)}, u32[]{:S(2)}) collective-permute-start(f32[2048]{0:T(1024)S(1)} %log_add_fusion.7), channel_id=1, source_target_pairs={{0,2},{1,3},{2,0},{3,1},{4,6},{5,7},{6,4},{7,5},{8,10},{9,11},{10,... | collective-permute-start | bytes 24584 | tf_op jit(solution)/shard_map/ppermute | solution.py:24
  52.5 2.1 %collective-permute-done.13 = f32[2048]{0:T(1024)S(1)} collective-permute-done((f32[2048]{0:T(1024)S(1)}, f32[2048]{0:T(1024)S(1)}, u32[]{:S(2)}, u32[]{:S(2)}) %collective-permute-start.13) | collective-permute-done | bytes 8224 | tf_op jit(solution)/shard_map/ppermute | solution.py:24
  54.6 1.6 %collective-permute-start.14 = (f32[2048]{0:T(1024)S(1)}, f32[2048]{0:T(1024)S(1)}, u32[]{:S(2)}, u32[]{:S(2)}) collective-permute-start(f32[2048]{0:T(1024)S(1)} %log_add_fusion.6), channel_id=1, source_target_pairs={{0,4},{1,5},{2,6},{3,7},{4,0},{5,1},{6,2},{7,3},{8,12},{9,13},{10,... | collective-permute-start | bytes 24584 | tf_op jit(solution)/shard_map/ppermute | solution.py:24
  56.2 2.1 %collective-permute-done.14 = f32[2048]{0:T(1024)S(1)} collective-permute-done((f32[2048]{0:T(1024)S(1)}, f32[2048]{0:T(1024)S(1)}, u32[]{:S(2)}, u32[]{:S(2)}) %collective-permute-start.14) | collective-permute-done | bytes 8224 | tf_op jit(solution)/shard_map/ppermute | solution.py:24
  59.8 1.2 %exponential_reduce_fusion.3 = f32[2048]{0:T(1024)S(1)} fusion(f32[2048,512]{1,0:T(8,128)S(1)} %get-tuple-element.23, f32[2048]{0:T(1024)S(1)} %add_reduce_fusion.1, f32[512]{0:T(512)S(1)} %subtract_multiply_fusion.6), kind=kLoop, calls=%fused_computation.3 | loop fusion | flops 3143680 | bytes 4212736 | tf_op jit(solution)/shard_map/reduce_sum | solution.py:100
  62.4 1.6 %collective-permute-start.16 = (f32[2048]{0:T(1024)S(1)}, f32[2048]{0:T(1024)S(1)}, u32[]{:S(2)}, u32[]{:S(2)}) collective-permute-start(f32[2048]{0:T(1024)S(1)} %log_add_fusion.4), channel_id=1, source_target_pairs={{0,2},{1,3},{2,0},{3,1},{4,6},{5,7},{6,4},{7,5},{8,10},{9,11},{10,... | collective-permute-start | bytes 24584 | tf_op jit(solution)/shard_map/ppermute | solution.py:24
  64.0 2.1 %collective-permute-done.16 = f32[2048]{0:T(1024)S(1)} collective-permute-done((f32[2048]{0:T(1024)S(1)}, f32[2048]{0:T(1024)S(1)}, u32[]{:S(2)}, u32[]{:S(2)}) %collective-permute-start.16) | collective-permute-done | bytes 8224 | tf_op jit(solution)/shard_map/ppermute | solution.py:24
  66.1 1.6 %collective-permute-start.17 = (f32[2048]{0:T(1024)S(1)}, f32[2048]{0:T(1024)S(1)}, u32[]{:S(2)}, u32[]{:S(2)}) collective-permute-start(f32[2048]{0:T(1024)S(1)} %log_add_fusion.3), channel_id=1, source_target_pairs={{0,4},{1,5},{2,6},{3,7},{4,0},{5,1},{6,2},{7,3},{8,12},{9,13},{10,... | collective-permute-start | bytes 24584 | tf_op jit(solution)/shard_map/ppermute | solution.py:24
  67.7 2.1 %collective-permute-done.17 = f32[2048]{0:T(1024)S(1)} collective-permute-done((f32[2048]{0:T(1024)S(1)}, f32[2048]{0:T(1024)S(1)}, u32[]{:S(2)}, u32[]{:S(2)}) %collective-permute-start.17) | collective-permute-done | bytes 8224 | tf_op jit(solution)/shard_map/ppermute | solution.py:24
  71.3 1.2 %exponential_reduce_fusion.1 = f32[2048]{0:T(1024)S(1)} fusion(f32[2048,512]{1,0:T(8,128)S(1)} %get-tuple-element.23, f32[2048]{0:T(1024)S(1)} %add_reduce_fusion, f32[512]{0:T(512)S(1)} %subtract_multiply_fusion.5), kind=kLoop, calls=%fused_computation.1 | loop fusion | flops 3143680 | bytes 4212736 | tf_op jit(solution)/shard_map/reduce_sum | solution.py:100
  72.6 1.2 %collective-permute-done.18 = f32[2048]{0:T(1024)S(1)} collective-permute-done((f32[2048]{0:T(1024)S(1)}, f32[2048]{0:T(1024)S(1)}, u32[]{:S(2)}, u32[]{:S(2)}) %collective-permute-start.18) | collective-permute-done | bytes 8224 | tf_op jit(solution)/shard_map/ppermute | solution.py:24
  73.7 1.6 %collective-permute-start.19 = (f32[2048]{0:T(1024)S(1)}, f32[2048]{0:T(1024)S(1)}, u32[]{:S(2)}, u32[]{:S(2)}) collective-permute-start(f32[2048]{0:T(1024)S(1)} %log_add_fusion.1), channel_id=1, source_target_pairs={{0,2},{1,3},{2,0},{3,1},{4,6},{5,7},{6,4},{7,5},{8,10},{9,11},{10,... | collective-permute-start | bytes 24584 | tf_op jit(solution)/shard_map/ppermute | solution.py:24
  75.3 2.1 %collective-permute-done.19 = f32[2048]{0:T(1024)S(1)} collective-permute-done((f32[2048]{0:T(1024)S(1)}, f32[2048]{0:T(1024)S(1)}, u32[]{:S(2)}, u32[]{:S(2)}) %collective-permute-start.19) | collective-permute-done | bytes 8224 | tf_op jit(solution)/shard_map/ppermute | solution.py:24
  77.5 1.6 %collective-permute-start.20 = (f32[2048]{0:T(1024)S(1)}, f32[2048]{0:T(1024)S(1)}, u32[]{:S(2)}, u32[]{:S(2)}) collective-permute-start(f32[2048]{0:T(1024)S(1)} %log_add_fusion), channel_id=1, source_target_pairs={{0,4},{1,5},{2,6},{3,7},{4,0},{5,1},{6,2},{7,3},{8,12},{9,13},{10,... | collective-permute-start | bytes 24584 | tf_op jit(solution)/shard_map/ppermute | solution.py:24
  79.1 2.1 %collective-permute-done.20 = f32[2048]{0:T(1024)S(1)} collective-permute-done((f32[2048]{0:T(1024)S(1)}, f32[2048]{0:T(1024)S(1)}, u32[]{:S(2)}, u32[]{:S(2)}) %collective-permute-start.20) | collective-permute-done | bytes 8224 | tf_op jit(solution)/shard_map/ppermute | solution.py:24
  (77 shorter events, 18.0 us)
Async XLA Ops:
  0.6 7.4 %copy-start = (bf16[512,512]{1,0:T(8,128)(2,1)S(1)}, bf16[512,512]{1,0:T(8,128)(2,1)}, u32[]{:S(2)}) copy-start(bf16[512,512]{1,0:T(8,128)(2,1)} %param.5) | copy-start | bytes 1572868
  0.6 32.1 %copy-start.1 = (bf16[50,512]{1,0:T(8,128)(2,1)S(1)}, bf16[50,512]{1,0:T(8,128)(2,1)}, u32[]{:S(2)}) copy-start(bf16[50,512]{1,0:T(8,128)(2,1)} %param.7) | copy-start | bytes 153604
  2.3 7.5 %collective-permute-start.5 = (f32[51,256]{1,0:T(8,128)S(1)}, f32[51,256]{1,0:T(8,128)S(1)}, u32[]{:S(2)}, u32[]{:S(2)}) collective-permute-start(f32[51,256]{1,0:T(8,128)S(1)} %fusion.7), channel_id=1, source_target_pairs={{0,24},{8,16},{16,8},{24,0},{1,25},{9,17},{17,9},{25,1},{2,26},{10... | collective-permute-start | bytes 156680 | tf_op jit(solution)/shard_map/ppermute | solution.py:62
  7.4 5.1 %collective-permute-start.4 = (f32[51,256]{1,0:T(8,128)S(1)}, f32[51,256]{1,0:T(8,128)S(1)}, u32[]{:S(2)}, u32[]{:S(2)}) collective-permute-start(f32[51,256]{1,0:T(8,128)S(1)} %fusion.7), channel_id=1, source_target_pairs={{0,16},{8,24},{16,0},{24,8},{1,17},{9,25},{17,1},{25,9},{2,18},{10... | collective-permute-start | bytes 156680 | tf_op jit(solution)/shard_map/ppermute | solution.py:62
  7.4 5.1 %collective-permute-start.3 = (f32[51,256]{1,0:T(8,128)S(1)}, f32[51,256]{1,0:T(8,128)S(1)}, u32[]{:S(2)}, u32[]{:S(2)}) collective-permute-start(f32[51,256]{1,0:T(8,128)S(1)} %fusion.7), channel_id=1, source_target_pairs={{0,8},{8,0},{16,24},{24,16},{1,9},{9,1},{17,25},{25,17},{2,10},{10... | collective-permute-start | bytes 156680 | tf_op jit(solution)/shard_map/ppermute | solution.py:62
  12.5 10.3 %collective-permute-start.6 = (f32[204,256]{1,0:T(8,128)S(1)}, f32[204,256]{1,0:T(8,128)S(1)}, u32[]{:S(2)}, u32[]{:S(2)}) collective-permute-start(f32[204,256]{1,0:T(8,128)S(1)} %pad_maximum_fusion.1), channel_id=1, source_target_pairs={{0,1},{1,0},{2,3},{3,2},{4,5},{5,4},{6,7},{7,6},{8,9},{9,8},{10,11... | collective-permute-start | bytes 626696 | tf_op jit(solution)/shard_map/ppermute | solution.py:77
  13.6 1.4 %collective-permute-start = (f32[50,50]{1,0:T(8,128)S(1)}, f32[50,50]{1,0:T(8,128)S(1)}, u32[]{:S(2)}, u32[]{:S(2)}) collective-permute-start(f32[50,50]{1,0:T(8,128)S(1)} %fusion.38), channel_id=1, source_target_pairs={{0,1},{1,0},{2,3},{3,2},{4,5},{5,4},{6,7},{7,6},{8,9},{9,8},{10,11... | collective-permute-start | bytes 30008 | tf_op jit(solution)/shard_map/ppermute | solution.py:24
  15.0 3.9 %collective-permute-start.1 = (f32[50,50]{1,0:T(8,128)S(1)}, f32[50,50]{1,0:T(8,128)S(1)}, u32[]{:S(2)}, u32[]{:S(2)}) collective-permute-start(f32[50,50]{1,0:T(8,128)S(1)} %add.257), channel_id=1, source_target_pairs={{0,2},{1,3},{2,0},{3,1},{4,6},{5,7},{6,4},{7,5},{8,10},{9,11},{10,... | collective-permute-start | bytes 30008 | tf_op jit(solution)/shard_map/ppermute | solution.py:24
  18.9 3.9 %collective-permute-start.2 = (f32[50,50]{1,0:T(8,128)S(1)}, f32[50,50]{1,0:T(8,128)S(1)}, u32[]{:S(2)}, u32[]{:S(2)}) collective-permute-start(f32[50,50]{1,0:T(8,128)S(1)} %add.258), channel_id=1, source_target_pairs={{0,4},{1,5},{2,6},{3,7},{4,0},{5,1},{6,2},{7,3},{8,12},{9,13},{10,... | collective-permute-start | bytes 30008 | tf_op jit(solution)/shard_map/ppermute | solution.py:24
  22.7 3.9 %collective-permute-start.7 = (f32[50,50]{1,0:T(8,128)S(1)}, f32[50,50]{1,0:T(8,128)S(1)}, u32[]{:S(2)}, u32[]{:S(2)}) collective-permute-start(f32[50,50]{1,0:T(8,128)S(1)} %add.259), channel_id=1, source_target_pairs={{0,8},{8,0},{16,24},{24,16},{1,9},{9,1},{17,25},{25,17},{2,10},{10... | collective-permute-start | bytes 30008 | tf_op jit(solution)/shard_map/ppermute | solution.py:24
  26.7 4.8 %collective-permute-start.8 = (f32[50,50]{1,0:T(8,128)S(1)}, f32[50,50]{1,0:T(8,128)S(1)}, u32[]{:S(2)}, u32[]{:S(2)}) collective-permute-start(f32[50,50]{1,0:T(8,128)S(1)} %add.261), channel_id=1, source_target_pairs={{0,16},{8,24},{16,0},{24,8},{1,17},{9,25},{17,1},{25,9},{2,18},{10... | collective-permute-start | bytes 30008 | tf_op jit(solution)/shard_map/ppermute | solution.py:24
  38.2 1.2 %collective-permute-start.9 = (f32[2048]{0:T(1024)S(1)}, f32[2048]{0:T(1024)S(1)}, u32[]{:S(2)}, u32[]{:S(2)}) collective-permute-start(f32[2048]{0:T(1024)S(1)} %log_add_fusion.11), channel_id=1, source_target_pairs={{0,1},{1,0},{2,3},{3,2},{4,5},{5,4},{6,7},{7,6},{8,9},{9,8},{10,11... | collective-permute-start | bytes 24584 | tf_op jit(solution)/shard_map/ppermute | solution.py:24
  39.5 3.7 %collective-permute-start.10 = (f32[2048]{0:T(1024)S(1)}, f32[2048]{0:T(1024)S(1)}, u32[]{:S(2)}, u32[]{:S(2)}) collective-permute-start(f32[2048]{0:T(1024)S(1)} %log_add_fusion.10), channel_id=1, source_target_pairs={{0,2},{1,3},{2,0},{3,1},{4,6},{5,7},{6,4},{7,5},{8,10},{9,11},{10,... | collective-permute-start | bytes 24584 | tf_op jit(solution)/shard_map/ppermute | solution.py:24
  43.2 3.7 %collective-permute-start.11 = (f32[2048]{0:T(1024)S(1)}, f32[2048]{0:T(1024)S(1)}, u32[]{:S(2)}, u32[]{:S(2)}) collective-permute-start(f32[2048]{0:T(1024)S(1)} %log_add_fusion.9), channel_id=1, source_target_pairs={{0,4},{1,5},{2,6},{3,7},{4,0},{5,1},{6,2},{7,3},{8,12},{9,13},{10,... | collective-permute-start | bytes 24584 | tf_op jit(solution)/shard_map/ppermute | solution.py:24
  47.4 0.7 copy-start.2
  49.6 1.2 %collective-permute-start.12 = (f32[2048]{0:T(1024)S(1)}, f32[2048]{0:T(1024)S(1)}, u32[]{:S(2)}, u32[]{:S(2)}) collective-permute-start(f32[2048]{0:T(1024)S(1)} %log_add_fusion.8), channel_id=1, source_target_pairs={{0,1},{1,0},{2,3},{3,2},{4,5},{5,4},{6,7},{7,6},{8,9},{9,8},{10,11... | collective-permute-start | bytes 24584 | tf_op jit(solution)/shard_map/ppermute | solution.py:24
  50.9 3.7 %collective-permute-start.13 = (f32[2048]{0:T(1024)S(1)}, f32[2048]{0:T(1024)S(1)}, u32[]{:S(2)}, u32[]{:S(2)}) collective-permute-start(f32[2048]{0:T(1024)S(1)} %log_add_fusion.7), channel_id=1, source_target_pairs={{0,2},{1,3},{2,0},{3,1},{4,6},{5,7},{6,4},{7,5},{8,10},{9,11},{10,... | collective-permute-start | bytes 24584 | tf_op jit(solution)/shard_map/ppermute | solution.py:24
  54.6 3.7 %collective-permute-start.14 = (f32[2048]{0:T(1024)S(1)}, f32[2048]{0:T(1024)S(1)}, u32[]{:S(2)}, u32[]{:S(2)}) collective-permute-start(f32[2048]{0:T(1024)S(1)} %log_add_fusion.6), channel_id=1, source_target_pairs={{0,4},{1,5},{2,6},{3,7},{4,0},{5,1},{6,2},{7,3},{8,12},{9,13},{10,... | collective-permute-start | bytes 24584 | tf_op jit(solution)/shard_map/ppermute | solution.py:24
  61.0 1.4 %collective-permute-start.15 = (f32[2048]{0:T(1024)S(1)}, f32[2048]{0:T(1024)S(1)}, u32[]{:S(2)}, u32[]{:S(2)}) collective-permute-start(f32[2048]{0:T(1024)S(1)} %log_add_fusion.5), channel_id=1, source_target_pairs={{0,1},{1,0},{2,3},{3,2},{4,5},{5,4},{6,7},{7,6},{8,9},{9,8},{10,11... | collective-permute-start | bytes 24584 | tf_op jit(solution)/shard_map/ppermute | solution.py:24
  62.4 3.7 %collective-permute-start.16 = (f32[2048]{0:T(1024)S(1)}, f32[2048]{0:T(1024)S(1)}, u32[]{:S(2)}, u32[]{:S(2)}) collective-permute-start(f32[2048]{0:T(1024)S(1)} %log_add_fusion.4), channel_id=1, source_target_pairs={{0,2},{1,3},{2,0},{3,1},{4,6},{5,7},{6,4},{7,5},{8,10},{9,11},{10,... | collective-permute-start | bytes 24584 | tf_op jit(solution)/shard_map/ppermute | solution.py:24
  66.1 3.7 %collective-permute-start.17 = (f32[2048]{0:T(1024)S(1)}, f32[2048]{0:T(1024)S(1)}, u32[]{:S(2)}, u32[]{:S(2)}) collective-permute-start(f32[2048]{0:T(1024)S(1)} %log_add_fusion.3), channel_id=1, source_target_pairs={{0,4},{1,5},{2,6},{3,7},{4,0},{5,1},{6,2},{7,3},{8,12},{9,13},{10,... | collective-permute-start | bytes 24584 | tf_op jit(solution)/shard_map/ppermute | solution.py:24
  72.5 1.2 %collective-permute-start.18 = (f32[2048]{0:T(1024)S(1)}, f32[2048]{0:T(1024)S(1)}, u32[]{:S(2)}, u32[]{:S(2)}) collective-permute-start(f32[2048]{0:T(1024)S(1)} %log_add_fusion.2), channel_id=1, source_target_pairs={{0,1},{1,0},{2,3},{3,2},{4,5},{5,4},{6,7},{7,6},{8,9},{9,8},{10,11... | collective-permute-start | bytes 24584 | tf_op jit(solution)/shard_map/ppermute | solution.py:24
  73.7 3.7 %collective-permute-start.19 = (f32[2048]{0:T(1024)S(1)}, f32[2048]{0:T(1024)S(1)}, u32[]{:S(2)}, u32[]{:S(2)}) collective-permute-start(f32[2048]{0:T(1024)S(1)} %log_add_fusion.1), channel_id=1, source_target_pairs={{0,2},{1,3},{2,0},{3,1},{4,6},{5,7},{6,4},{7,5},{8,10},{9,11},{10,... | collective-permute-start | bytes 24584 | tf_op jit(solution)/shard_map/ppermute | solution.py:24
  77.5 3.7 %collective-permute-start.20 = (f32[2048]{0:T(1024)S(1)}, f32[2048]{0:T(1024)S(1)}, u32[]{:S(2)}, u32[]{:S(2)}) collective-permute-start(f32[2048]{0:T(1024)S(1)} %log_add_fusion), channel_id=1, source_target_pairs={{0,4},{1,5},{2,6},{3,7},{4,0},{5,1},{6,2},{7,3},{8,12},{9,13},{10,... | collective-permute-start | bytes 24584 | tf_op jit(solution)/shard_map/ppermute | solution.py:24
  81.2 1.0 %copy-start.3 = (f32[512]{0:T(512)}, f32[512]{0:T(512)S(1)}, u32[]{:S(2)}) copy-start(f32[512]{0:T(512)S(1)} %slice.120) | copy-start | bytes 6148
  82.3 1.1 %copy-start.4 = (f32[512]{0:T(512)}, f32[512]{0:T(512)S(1)}, u32[]{:S(2)}) copy-start(f32[512]{0:T(512)S(1)} %subtract_multiply_fusion.4) | copy-start | bytes 6148
